TPU v7x, 32 devices: a whole 2x2x4 slice. The times are simulated.
32 devices in a mesh: row: 4 (over x, core), col: 8 (over z, y).
Axes of the slice: x: 2, y: 2, z: 4, core: 2. Of those that a mesh axis runs over, the one named last changes fastest.
Arguments:
- stiffness: bfloat16 [896, 256, 256], P(('row', 'col')), may hold values from -0.25 to 0.25
- stiffness_index: int32 [896, 2], P(('row', 'col')), may hold values from 0 to 15
- mode_basis: bfloat16 [131072, 256], P(('row', 'col')), may hold values from -0.75 to 0.75
- pair_owner: int32 [32, 2], replicated, may hold values from 0 to 1
- margin: int32 [32, 2, 4, 2], replicated, may hold values from 0 to 15
Outputs:
- coarse: bfloat16 [32, 32, 256, 256], P('row', None, 'col')
All inputs are finite; a program needn't handle non-finite values.
Results may differ from a plain program's by a relative error of at most 0.0049.
Values may be sent and summed in bfloat16 or wider, within the bound.
A program may use at most 128 MiB of HBM per device.

v0:
```python
import jax
import jax.numpy as jnp
from jax import lax
from jax.sharding import PartitionSpec as P


def from_behind(array, axis, by):
    count = lax.axis_size(axis)
    pairs = [(i, i + by) for i in range(count) if 0 <= i + by < count]
    return lax.ppermute(array, axis, pairs)


def gather_rows(blocks, picks):
    return blocks[picks].reshape(-1, blocks.shape[2])


def project(left, right):
    return jnp.einsum("nm,nk->mk", left, right, preferred_element_type=jnp.float32).astype(
        jnp.bfloat16
    )


def maybe_project(flag, left, right):
    return lax.cond(
        flag,
        lambda: project(left, right),
        lambda: jnp.zeros((left.shape[1], right.shape[1]), jnp.bfloat16),
    )


def on_device(stiffness, stiffness_index, mode_basis, pair_owner, margin):
    grid_rows = lax.axis_size("row")
    grid_cols = lax.axis_size("col")
    my_row = lax.axis_index("row")
    my_col = lax.axis_index("col")
    subdomain = my_row * grid_cols + my_col
    block_size = stiffness.shape[1]
    mode_count = mode_basis.shape[1]
    block_count = mode_basis.shape[0] // block_size
    mode_blocks = mode_basis.reshape(block_count, block_size, mode_count)
    picked = mode_blocks[stiffness_index[:, 1]]
    products = jnp.einsum("kab,kbm->kam", stiffness, picked, preferred_element_type=jnp.float32)
    selector = (stiffness_index[:, 0][None, :] == jnp.arange(block_count)[:, None]).astype(
        jnp.float32
    )
    summed = jnp.dot(
        selector, products.reshape(products.shape[0], -1), precision=lax.Precision.HIGHEST
    )
    applied = summed.astype(jnp.bfloat16).reshape(block_count, block_size, mode_count)
    diagonal = project(mode_basis, applied.reshape(-1, mode_count))
    has_next_col = my_col < grid_cols - 1
    has_next_row = my_row < grid_rows - 1
    prev_col = jnp.maximum(subdomain - 1, 0)
    prev_row = jnp.maximum(subdomain - grid_cols, 0)
    owner_next_col = pair_owner[subdomain, 0]
    owner_prev_col = pair_owner[prev_col, 0]
    owner_next_row = pair_owner[subdomain, 1]
    owner_prev_row = pair_owner[prev_row, 1]
    lists_next_col = margin[subdomain, 0]
    lists_prev_col = margin[prev_col, 0]
    lists_next_row = margin[subdomain, 1]
    lists_prev_row = margin[prev_row, 1]

    def far_rows(owner_flag, picks):
        return jnp.where(
            owner_flag == 0, gather_rows(applied, picks), gather_rows(mode_blocks, picks)
        )

    def near_rows(owner_flag, picks):
        return jnp.where(
            owner_flag == 0, gather_rows(mode_blocks, picks), gather_rows(applied, picks)
        )

    from_col = from_behind(far_rows(owner_prev_col, lists_prev_col[:, 1]), "col", -1)
    from_row = from_behind(far_rows(owner_prev_row, lists_prev_row[:, 1]), "row", -1)
    next_col_block = maybe_project(
        has_next_col, near_rows(owner_next_col, lists_next_col[:, 0]), from_col
    )
    row_block = maybe_project(
        has_next_row, near_rows(owner_next_row, lists_next_row[:, 0]), from_row
    )
    slots = jnp.stack([diagonal, next_col_block, row_block])
    row_shift = [0, 0, 0]
    col_offset = [0, 1, grid_cols]
    slot_count = slots.shape[0]
    part_rows = mode_count // grid_cols
    pieces = slots.reshape(slot_count, grid_cols, part_rows, mode_count)
    received = lax.all_to_all(pieces, "col", split_axis=1, concat_axis=1, tiled=True)
    sources = jnp.arange(grid_cols, dtype=jnp.int32)
    local_index = sources[None, :] + jnp.array(row_shift, jnp.int32)[:, None]
    local_index = jnp.where(local_index < 0, grid_cols, local_index)
    global_index = my_row * grid_cols + sources[None, :] + jnp.array(col_offset, jnp.int32)[:, None]
    total_subdomains = grid_rows * grid_cols
    stored = jnp.zeros((grid_cols, total_subdomains, part_rows, mode_count), jnp.bfloat16)
    return stored.at[local_index, global_index].add(received, mode="drop")


def solution(mesh):
    return jax.shard_map(
        on_device,
        mesh=mesh,
        in_specs=(
            P(("row", "col"), None, None),
            P(("row", "col"), None),
            P(("row", "col"), None),
            P(),
            P(),
        ),
        out_specs=P("row", None, "col", None),
        check_vma=False,
    )
```

profile of v0, /device:TPU:0, one launch (start us, length us, event | category | flops | bytes accessed | tf_op | source)
XLA Modules:
  0.0 96.7 jit_solution(13674847605289263204)
XLA Ops:
  0.0 0.8 constant_dynamic-slice_fusion.3
  0.8 0.1 copy.31
  0.9 0.1 copy.33
  1.1 0.8 slice_bitcast_fusion
  1.8 4.3 %gather_fusion.4 = bf16[28,256,256]{2,1,0:T(8,128)(2,1)} fusion(bf16[16,256,256]{2,1,0:T(8,128)(2,1)} %bitcast.56, s32[1024]{0:T(1024)S(1)} %pad_clamp_fusion.4), kind=kCustom, calls=%fused_computation.4 | custom fusion | bytes 7340144 | tf_op jit(solution)/shard_map/gather | solution.py:41
  6.1 7.3 %convolution_bitcast_fusion = f32[28,256,256]{1,2,0:T(8,128)} fusion(bf16[28,256,256]{2,1,0:T(8,128)(2,1)} %gather_fusion.4, bf16[28,256,256]{2,1,0:T(8,128)(2,1)} %param.11), kind=kOutput, calls=%fused_computation.23 | convolution fusion | flops 939524096 | bytes 14680064 | tf_op jit(solution)/shard_map/kab,kbm->kam/dot_general | solution.py:42
  13.4 8.4 %copy.29 = f32[28,256,256]{2,1,0:T(8,128)} copy(f32[28,256,256]{1,2,0:T(8,128)} %convolution_bitcast_fusion) | data formatting | bytes 14680064 | tf_op jit(solution)/shard_map/kab,kbm->kam/dot_general | solution.py:42
  21.7 4.0 %pad.12 = f32[32,256,256]{2,1,0:T(8,128)S(1)} pad(f32[28,256,256]{2,1,0:T(8,128)} %copy.29, f32[]{:T(128)} %constant.102), padding=0_4x0_0x0_0 | pad | bytes 15728644
  25.7 4.9 %copy.39 = f32[4,8,256,256]{3,1,2,0:T(8,128)S(1)} copy(f32[4,8,256,256]{3,2,1,0:T(8,128)S(1)} %bitcast.53) | data formatting | bytes 16777216
  30.6 3.1 %convolution_convert_fusion.2 = bf16[16,65536]{1,0:T(8,128)(2,1)S(1)} fusion(f32[28,65536]{1,0:T(8,128)S(1)} %bitcast.54, s32[28]{0:T(128)S(1)} %get-tuple-element.128), kind=kOutput, calls=%fused_computation.22 | convolution fusion | flops 353370560 | bytes 9437296 | tf_op jit(solution)/shard_map/dot_general | solution.py:46
  33.8 0.0 copy-start.1
  33.8 1.8 %copy.40 = bf16[2,8,256,256]{3,2,1,0:T(8,128)(2,1)} copy(bf16[2,8,256,256]{3,1,2,0:T(8,128)(2,1)S(1)} %bitcast.55) | data formatting | bytes 4194304
  35.6 2.2 %gather_fusion.6 = bf16[4,256,256]{2,1,0:T(8,128)(2,1)S(1)} fusion(bf16[16,256,256]{2,1,0:T(8,128)(2,1)} %bitcast.57, s32[1024]{0:T(1024)S(1)} %pad_clamp_fusion.3), kind=kCustom, calls=%fused_computation.6 | custom fusion | bytes 1048592 | tf_op jit(solution)/shard_map/gather | solution.py:14
  37.7 2.2 %gather_fusion.5 = bf16[4,256,256]{2,1,0:T(8,128)(2,1)S(1)} fusion(bf16[16,256,256]{2,1,0:T(8,128)(2,1)} %bitcast.61, s32[1024]{0:T(1024)S(1)} %pad_clamp_fusion.3), kind=kCustom, calls=%fused_computation.5 | custom fusion | bytes 1048592 | tf_op jit(solution)/shard_map/gather | solution.py:14
  39.9 0.6 constant_dynamic-slice_fusion.4
  41.2 0.8 broadcast_select_fusion.3
  42.0 1.3 %collective-permute-start = (bf16[1024,256]{1,0:T(8,128)(2,1)}, bf16[1024,256]{1,0:T(8,128)(2,1)}, u32[]{:S(2)}, u32[]{:S(2)}) collective-permute-start(bf16[1024,256]{1,0:T(8,128)(2,1)} %bitcast.19), channel_id=1, source_target_pairs={{1,0},{2,1},{3,2},{4,3},{5,4},{6,5},{7,6},{9,8},{10,9},{11,10},{12... | collective-permute-start | bytes 1572872 | tf_op jit(solution)/shard_map/ppermute | solution.py:10
  43.3 2.2 %gather_fusion.7 = bf16[4,256,256]{2,1,0:T(8,128)(2,1)S(1)} fusion(bf16[16,256,256]{2,1,0:T(8,128)(2,1)} %bitcast.62, s32[1024]{0:T(1024)S(1)} %pad_clamp_fusion.2), kind=kCustom, calls=%fused_computation.7 | custom fusion | bytes 1048592 | tf_op jit(solution)/shard_map/gather | solution.py:14
  45.5 2.2 %gather_fusion.8 = bf16[4,256,256]{2,1,0:T(8,128)(2,1)S(1)} fusion(bf16[16,256,256]{2,1,0:T(8,128)(2,1)} %bitcast.58, s32[1024]{0:T(1024)S(1)} %pad_clamp_fusion.2), kind=kCustom, calls=%fused_computation.8 | custom fusion | bytes 1048592 | tf_op jit(solution)/shard_map/gather | solution.py:14
  48.3 0.9 broadcast_select_fusion.2
  49.2 1.5 %collective-permute-start.1 = (bf16[1024,256]{1,0:T(8,128)(2,1)}, bf16[1024,256]{1,0:T(8,128)(2,1)}, u32[]{:S(2)}, u32[]{:S(2)}) collective-permute-start(bf16[1024,256]{1,0:T(8,128)(2,1)} %bitcast.25), channel_id=1, source_target_pairs={{8,0},{16,8},{24,16},{9,1},{17,9},{25,17},{10,2},{18,10},{26,18},{... | collective-permute-start | bytes 1572872 | tf_op jit(solution)/shard_map/ppermute | solution.py:10
  50.7 2.0 %reshape_reshape.3 = bf16[4096,256]{1,0:T(8,128)(2,1)} reshape(bf16[16,65536]{1,0:T(8,128)(2,1)S(1)} %convolution_convert_fusion.2) | data formatting | bytes 4194304 | tf_op jit(solution)/shard_map/reshape;reshape | solution.py:50
  52.7 0.1 copy.30
  52.8 0.1 copy.32
  52.9 3.3 %convolution_convert_fusion.3 = bf16[256,256]{0,1:T(8,128)(2,1)S(1)} fusion(bf16[4096,256]{1,0:T(8,128)(2,1)} %reshape_reshape.3, bf16[4096,256]{1,0:T(8,128)(2,1)} %param.13), kind=kOutput, calls=%fused_computation.24 | convolution fusion | flops 536936448 | bytes 4325376 | tf_op jit(solution)/shard_map/nm,nk->mk/dot_general | solution.py:18
  56.1 3.0 %collective-permute-done = bf16[1024,256]{1,0:T(8,128)(2,1)} collective-permute-done((bf16[1024,256]{1,0:T(8,128)(2,1)}, bf16[1024,256]{1,0:T(8,128)(2,1)}, u32[]{:S(2)}, u32[]{:S(2)}) %collective-permute-start) | collective-permute-done | bytes 524320 | tf_op jit(solution)/shard_map/ppermute | solution.py:10
  59.1 0.0 copy-done
  59.1 5.3 %conditional.2 = (bf16[1,8,32,256]{3,2,1,0:T(8,128)(2,1)S(1)}) conditional(s32[]{:T(128)} %convert_element_type.27, () %tuple.25, (s32[32,2]{0,1:T(2,128)S(1)}, s32[]{:T(128)}, bf16[16,256,256]{2,1,0:T(8,128)(2,1)S(1)}, s32[4,1]{0,1:T(1,128)S(1)}, bf16[16,256,256]{2,1,0:T(8,128)(2,1)}, /*index=5*/bf16[1024,256]{1,0:T(8,128)(2,1)}, ...), branch_computations={%region_0.1_spmd, %region_1.2_spmd} | conditional | flops 134546448 | bytes 4853910 | solution.py:24
  59.2 0.6 gather_fusion
  59.7 2.2 %gather_fusion.1 = bf16[4,256,256]{2,1,0:T(8,128)(2,1)S(1)} fusion(bf16[16,256,256]{2,1,0:T(8,128)(2,1)} %get-tuple-element.98, s32[1024]{0:T(1024)S(1)} %pad_clamp_fusion), kind=kCustom, calls=%fused_computation.1 | custom fusion | bytes 1048592 | tf_op jit(solution)/shard_map/gather | solution.py:14
  61.9 0.6 fusion.10
  62.5 0.6 broadcast_select_fusion
  63.1 1.4 %convolution_convert_fusion = bf16[256,256]{1,0:T(8,128)(2,1)S(1)} fusion(bf16[1024,256]{1,0:T(8,128)(2,1)S(1)} %bitcast.66, bf16[1024,256]{1,0:T(8,128)(2,1)} %get-tuple-element.99), kind=kOutput, calls=%fused_computation.10 | convolution fusion | flops 134283264 | bytes 1179648 | tf_op jit(solution)/shard_map/cond/branch_1_fun/nm,nk->mk/dot_general | solution.py:18
  64.5 0.0 copy-start.2
  64.5 0.0 collective-permute-done.1
  64.5 5.4 %conditional.3 = (bf16[1,8,32,256]{3,2,1,0:T(8,128)(2,1)S(1)}) conditional(s32[]{:T(128)} %convert_element_type.28, () %tuple.27, (s32[32,2]{0,1:T(2,128)S(1)}, s32[]{:T(128)}, bf16[16,256,256]{2,1,0:T(8,128)(2,1)S(1)}, s32[4,1]{0,1:T(1,128)S(1)}, bf16[16,256,256]{2,1,0:T(8,128)(2,1)}, /*index=5*/bf16[1024,256]{1,0:T(8,128)(2,1)}, ...), branch_computations={%region_2.3_spmd, %region_3.4_spmd} | conditional | flops 134546448 | bytes 4853910 | solution.py:24
  64.6 0.6 gather_fusion.2
  65.2 2.2 %gather_fusion.3 = bf16[4,256,256]{2,1,0:T(8,128)(2,1)S(1)} fusion(bf16[16,256,256]{2,1,0:T(8,128)(2,1)} %get-tuple-element.104, s32[1024]{0:T(1024)S(1)} %pad_clamp_fusion.1), kind=kCustom, calls=%fused_computation.3 | custom fusion | bytes 1048592 | tf_op jit(solution)/shard_map/gather | solution.py:14
  67.3 0.6 fusion.11
  67.9 0.6 broadcast_select_fusion.1
  68.5 1.4 %convolution_convert_fusion.1 = bf16[256,256]{1,0:T(8,128)(2,1)S(1)} fusion(bf16[1024,256]{1,0:T(8,128)(2,1)S(1)} %bitcast.67, bf16[1024,256]{1,0:T(8,128)(2,1)} %get-tuple-element.105), kind=kOutput, calls=%fused_computation.16 | convolution fusion | flops 134283264 | bytes 1179648 | tf_op jit(solution)/shard_map/cond/branch_1_fun/nm,nk->mk/dot_general | solution.py:18
  69.9 0.8 pad_maximum_fusion
  70.7 5.9 %all-to-all-start = ((bf16[3,8,32,256]{3,2,0,1:T(8,128)(2,1)}), bf16[3,8,32,256]{3,2,0,1:T(8,128)(2,1)S(1)}, u32[]{:S(2)}, u32[]{:S(2)}) async-start(bf16[3,8,32,256]{3,2,0,1:T(8,128)(2,1)} %pad_maximum_fusion), calls=%async_computation | async-start | bytes 786432 | tf_op jit(solution)/shard_map/all_to_all | solution.py:88
  76.7 0.1 fusion.5
  76.8 0.1 reshape.234
  76.8 12.3 %all-to-all-done = bf16[3,8,32,256]{3,2,0,1:T(8,128)(2,1)S(1)} async-done(((bf16[3,8,32,256]{3,2,0,1:T(8,128)(2,1)}), bf16[3,8,32,256]{3,2,0,1:T(8,128)(2,1)S(1)}, u32[]{:S(2)}, u32[]{:S(2)}) %all-to-all-start) | async-done | bytes 393248 | tf_op jit(solution)/shard_map/all_to_all | solution.py:88
  89.1 2.5 %broadcast_in_dim.5 = bf16[8,32,32,256]{3,2,1,0:T(8,128)(2,1)} broadcast(bf16[]{:T(256)} %constant.16.clone.1), dimensions={} | broadcast | bytes 4194306 | tf_op jit(solution)/shard_map/broadcast_in_dim | solution.py:94
  91.7 5.0 %scatter_fusion = bf16[8,32,32,256]{3,2,1,0:T(8,128)(2,1)} fusion(bf16[8,32,32,256]{3,2,1,0:T(8,128)(2,1)} %broadcast_in_dim.5, s32[24]{0:T(128)S(1)} %reshape.234, bf16[24,32,256]{2,1,0:T(8,128)(2,1)S(1)} %bitcast.65), kind=kCustom, calls=%fused_computation.9 | custom fusion | flops 196608 | bytes 1179840 | tf_op jit(solution)/shard_map/scatter-add | solution.py:95
  (16 shorter events, 0.1 us)
Async XLA Ops:
  33.8 6.2 %copy-start.1 = (s32[32,2]{0,1:T(2,128)S(1)}, s32[32,2]{0,1:T(2,128)}, u32[]{:S(2)}) copy-start(s32[32,2]{0,1:T(2,128)} %param.14) | copy-start | bytes 772
  42.0 17.1 %collective-permute-start = (bf16[1024,256]{1,0:T(8,128)(2,1)}, bf16[1024,256]{1,0:T(8,128)(2,1)}, u32[]{:S(2)}, u32[]{:S(2)}) collective-permute-start(bf16[1024,256]{1,0:T(8,128)(2,1)} %bitcast.19), channel_id=1, source_target_pairs={{1,0},{2,1},{3,2},{4,3},{5,4},{6,5},{7,6},{9,8},{10,9},{11,10},{12... | collective-permute-start | bytes 1572872 | tf_op jit(solution)/shard_map/ppermute | solution.py:10
  49.2 15.3 %collective-permute-start.1 = (bf16[1024,256]{1,0:T(8,128)(2,1)}, bf16[1024,256]{1,0:T(8,128)(2,1)}, u32[]{:S(2)}, u32[]{:S(2)}) collective-permute-start(bf16[1024,256]{1,0:T(8,128)(2,1)} %bitcast.25), channel_id=1, source_target_pairs={{8,0},{16,8},{24,16},{9,1},{17,9},{25,17},{10,2},{18,10},{26,18},{... | collective-permute-start | bytes 1572872 | tf_op jit(solution)/shard_map/ppermute | solution.py:10
  52.7 6.5 %copy-start = (bf16[4096,256]{1,0:T(8,128)(2,1)S(1)}, bf16[4096,256]{1,0:T(8,128)(2,1)}, u32[]{:S(2)}) copy-start(bf16[4096,256]{1,0:T(8,128)(2,1)} %param.13) | copy-start | bytes 6291460
  64.5 12.2 %copy-start.2 = (s32[3]{0:T(128)S(1)}, s32[3]{0:T(128)}, u32[]{:S(2)}) copy-start(s32[3]{0:T(128)} %constant.51.clone) | copy-start | bytes 40
  70.7 18.4 %all-to-all-start = ((bf16[3,8,32,256]{3,2,0,1:T(8,128)(2,1)}), bf16[3,8,32,256]{3,2,0,1:T(8,128)(2,1)S(1)}, u32[]{:S(2)}, u32[]{:S(2)}) async-start(bf16[3,8,32,256]{3,2,0,1:T(8,128)(2,1)} %pad_maximum_fusion), calls=%async_computation | async-start | bytes 786432 | tf_op jit(solution)/shard_map/all_to_all | solution.py:88
where the time goes:
time: 97.6 us; the launch traced here: 96.7 us
  local copies, waits for them, and re-layouts  44 us (45%)
  matrix products  16.4 us (17%)
  waiting for transfers between devices  15.3 us (16%)
  other arithmetic  10.8 us (11%)
  starting transfers between devices  8.67 us (9%)
  between operations  1.45 us (1%)
    gather x8, local copies, waits for them, and re-layouts, gather_rows(): return blocks[picks].reshape(-1, blocks.shape[2])  14.2 us
    all_to_all x1, waiting for transfers between devices, on_device(): lax.all_to_all(pieces, 'col', split_axis=1, concat_axis=1, tiled=True)  12.3 us
    unnamed x9, local copies, waits for them, and re-layouts  10.7 us
    dot_general x1, local copies, waits for them, and re-layouts, on_device(): jnp.einsum('kab,kbm->kam', stiffness, picked, preferred_element_type=jnp....  8.36 us
    dot_general x1, matrix products, on_device(): jnp.einsum('kab,kbm->kam', stiffness, picked, preferred_element_type=jnp....  7.27 us
    dot_general x3, matrix products, project(): jnp.einsum('nm,nk->mk', left, right, preferred_element_type=jnp.float32)  6.03 us
    all_to_all x1, starting transfers between devices, on_device(): lax.all_to_all(pieces, 'col', split_axis=1, concat_axis=1, tiled=True)  5.93 us
    scatter-add x1, other arithmetic, on_device(): return stored.at[local_index, global_index].add(received, mode='drop')  5.01 us
  transfers between devices with their start and end apart: 3, of which 2 were waited for; matrix products, arithmetic and copies ran while one was open for 17% of the time, Pallas kernels for 0%

commit v1 on v0

v1 whole, which is shorter than its diff:
```python
import functools

import jax
import jax.numpy as jnp
from jax import lax
from jax.experimental import pallas as pl
from jax.experimental.pallas import tpu as pltpu
from jax.sharding import PartitionSpec as P

MESH = pl.DeviceIdType.MESH
F32 = jnp.float32
BF16 = jnp.bfloat16


def tdot(left, right):
    return lax.dot_general(left, right, (((0,), (0,)), ((), ())), preferred_element_type=F32)


def exchange_kernel(
    n_row, n_col, group,
    table, index, owner, margin, stiff_hbm, modes_hbm, out,
    stiff, modes, sums, applied, far_out, far_in, slots, held, total,
    stiff_sem, modes_sem, far_send, far_recv, piece_send, piece_recv,
):
    block_total, size, width = stiff.shape
    blocks = modes.shape[0]
    shared = far_out.shape[1]
    my_row = lax.axis_index("row")
    my_col = lax.axis_index("col")
    here = my_row * n_col + my_col
    has_next = (my_col < n_col - 1, my_row < n_row - 1)
    has_prev = (my_col > 0, my_row > 0)
    prev_id = ({"col": jnp.maximum(my_col - 1, 0)}, {"row": jnp.maximum(my_row - 1, 0)})
    next_row = {"row": jnp.minimum(my_row + 1, n_row - 1)}

    modes_copy = pltpu.make_async_copy(modes_hbm, modes, modes_sem)
    modes_copy.start()

    def stiff_copy(c):
        part = pl.ds(c * group, group)
        return pltpu.make_async_copy(stiff_hbm.at[part], stiff.at[part], stiff_sem.at[c])

    def start_stiff(c, carry):
        stiff_copy(c).start()
        return carry

    lax.fori_loop(0, block_total // group, start_stiff, 0)

    barrier = pltpu.get_barrier_semaphore()
    for d in range(1, n_col):
        pl.semaphore_signal(
            barrier, inc=1, device_id={"col": lax.rem(my_col + d, n_col)}, device_id_type=MESH
        )

    @pl.when(has_prev[1])
    def _():
        pl.semaphore_signal(barrier, inc=1, device_id=prev_id[1], device_id_type=MESH)

    @pl.when(has_next[1])
    def _():
        pl.semaphore_signal(barrier, inc=1, device_id=next_row, device_id_type=MESH)

    sums[0] = jnp.zeros((size, width), F32)
    modes_copy.wait()

    def apply_group(c, carry):
        stiff_copy(c).wait()
        for q in range(group):
            k = c * group + q
            product = jnp.dot(stiff[k], modes[index[1, k]], preferred_element_type=F32)
            sums[k + 1] = sums[table[k]] + product
        return carry

    lax.fori_loop(0, block_total // group, apply_group, 0)

    sides = has_prev[1].astype(jnp.int32) + has_next[1].astype(jnp.int32)
    pl.semaphore_wait(barrier, n_col - 1 + sides)

    def far_copy(d, i):
        return pltpu.make_async_remote_copy(
            src_ref=far_out.at[d, i], dst_ref=far_in.at[d, i],
            send_sem=far_send.at[d, i], recv_sem=far_recv.at[d, i],
            device_id=prev_id[d], device_id_type=MESH,
        )

    for d in range(2):
        @pl.when(has_prev[d])
        def _():
            first = here - (1 if d == 0 else n_col)
            flag = owner[d, first]
            for i in range(shared):
                pick = margin[d, i, 1, first]
                far_out[d, i] = jnp.where(
                    flag == 0, sums[table[block_total + pick]].astype(BF16), modes[pick]
                )
                far_copy(d, i).start()

    def piece_copy(slot, d):
        return pltpu.make_async_remote_copy(
            src_ref=slots.at[slot, lax.rem(my_col + d, n_col)], dst_ref=held.at[slot, my_col],
            send_sem=piece_send.at[slot, d], recv_sem=piece_recv.at[slot, d],
            device_id={"col": lax.rem(my_col + d, n_col)}, device_id_type=MESH,
        )

    def scatter(slot, value):
        slots[slot] = value.astype(BF16).reshape(slots.shape[1:])
        for d in range(1, n_col):
            piece_copy(slot, d).start()
        held[slot, my_col] = slots[slot, my_col]

    def round_block(a, carry):
        applied[a] = sums[table[block_total + a]].astype(BF16)
        return carry

    lax.fori_loop(0, blocks, round_block, 0)
    step = 4 if blocks % 4 == 0 else 1
    total[...] = jnp.zeros_like(total)

    def diagonal_step(c, carry):
        part = pl.ds(c * step, step)
        total[...] += tdot(
            modes[part].reshape(step * size, width), applied[part].reshape(step * size, width)
        )
        return carry

    lax.fori_loop(0, blocks // step, diagonal_step, 0)
    scatter(0, total[...])

    for d in (1, 0):
        @pl.when(has_next[d])
        def _():
            flag = owner[d, here]
            value = None
            for i in range(shared):
                pick = margin[d, i, 0, here]
                near = jnp.where(flag == 0, modes[pick], applied[pick])
                far_copy(d, i).wait_recv()
                term = tdot(near, far_in[d, i])
                value = term if value is None else value + term
            scatter(d + 1, value)

    @pl.when(jnp.logical_not(has_next[1]))
    def _():
        held[2] = jnp.zeros(held.shape[1:], BF16)

    held[1, n_col - 1] = jnp.zeros(held.shape[2:], BF16)

    for d in range(2):
        @pl.when(has_prev[d])
        def _():
            for i in range(shared):
                far_copy(d, i).wait_send()

    def wait_piece(slot, d):
        source = lax.rem(my_col + n_col - d, n_col)
        return pltpu.make_async_remote_copy(
            src_ref=slots.at[slot, my_col], dst_ref=held.at[slot, source],
            send_sem=piece_send.at[slot, d], recv_sem=piece_recv.at[slot, d],
            device_id={"col": lax.rem(my_col + d, n_col)}, device_id_type=MESH,
        )

    for d in range(1, n_col):
        wait_piece(0, d).wait_recv()
        piece_copy(0, d).wait_send()

    @pl.when(has_next[1])
    def _():
        for d in range(1, n_col):
            wait_piece(2, d).wait_recv()
            piece_copy(2, d).wait_send()

    for d in range(1, n_col):
        @pl.when(lax.rem(my_col + n_col - d, n_col) < n_col - 1)
        def _():
            wait_piece(1, d).wait_recv()

        @pl.when(has_next[0])
        def _():
            piece_copy(1, d).wait_send()

    out[...] = held[...]


def place_kernel(n_row, n_col, held, out):
    i = pl.program_id(0)
    my_row = lax.axis_index("row")
    out[...] = jnp.zeros_like(out)
    spot = my_row * n_col + i
    out[0, spot] = held[0, i]

    @pl.when(i < n_col - 1)
    def _():
        out[0, spot + 1] = held[1, i]

    @pl.when(my_row < n_row - 1)
    def _():
        out[0, spot + n_col] = held[2, i]


def on_device(stiffness, stiffness_index, mode_basis, pair_owner, margin):
    n_row = lax.axis_size("row")
    n_col = lax.axis_size("col")
    count, size, _ = stiffness.shape
    width = mode_basis.shape[1]
    blocks = mode_basis.shape[0] // size
    shared = margin.shape[2]
    rows = width // n_col
    group = 4 if count % 4 == 0 else 1
    mine = stiffness_index[:, 0]
    number = jnp.arange(count, dtype=jnp.int32)
    wanted = jnp.concatenate([mine, jnp.arange(blocks, dtype=jnp.int32)])
    limit = jnp.concatenate([number, jnp.full((blocks,), count, jnp.int32)])
    match = (wanted[:, None] == mine[None, :]) & (number[None, :] < limit[:, None])
    table = jnp.max(jnp.where(match, number[None, :] + 1, 0), axis=1)

    smem = pl.BlockSpec(memory_space=pltpu.SMEM)
    hbm = pl.BlockSpec(memory_space=pl.ANY)
    held = pl.pallas_call(
        functools.partial(exchange_kernel, n_row, n_col, group),
        out_shape=jax.ShapeDtypeStruct((3, n_col, rows, width), BF16),
        in_specs=[smem] * 4 + [hbm] * 2,
        out_specs=pl.BlockSpec(memory_space=pltpu.VMEM),
        scratch_shapes=[
            pltpu.VMEM((count, size, size), BF16),
            pltpu.VMEM((blocks, size, width), BF16),
            pltpu.VMEM((count + 1, size, width), F32),
            pltpu.VMEM((blocks, size, width), BF16),
            pltpu.VMEM((2, shared, size, width), BF16),
            pltpu.VMEM((2, shared, size, width), BF16),
            pltpu.VMEM((3, n_col, rows, width), BF16),
            pltpu.VMEM((3, n_col, rows, width), BF16),
            pltpu.VMEM((width, width), F32),
            pltpu.SemaphoreType.DMA((count // group,)),
            pltpu.SemaphoreType.DMA,
            pltpu.SemaphoreType.DMA((2, shared)),
            pltpu.SemaphoreType.DMA((2, shared)),
            pltpu.SemaphoreType.DMA((3, n_col)),
            pltpu.SemaphoreType.DMA((3, n_col)),
        ],
        compiler_params=pltpu.CompilerParams(
            collective_id=0, has_side_effects=True, vmem_limit_bytes=56 * 1024 * 1024
        ),
        name="exchange",
    )(
        table,
        stiffness_index.T,
        pair_owner.T,
        margin.transpose(1, 2, 3, 0),
        stiffness,
        mode_basis.reshape(blocks, size, width),
    )
    places = n_row * n_col
    return pl.pallas_call(
        functools.partial(place_kernel, n_row, n_col),
        out_shape=jax.ShapeDtypeStruct((n_col, places, rows, width), BF16),
        grid=(n_col,),
        in_specs=[pl.BlockSpec((3, n_col, rows, width), lambda i: (0, 0, 0, 0))],
        out_specs=pl.BlockSpec((1, places, rows, width), lambda i: (i, 0, 0, 0)),
        compiler_params=pltpu.CompilerParams(vmem_limit_bytes=40 * 1024 * 1024),
        name="place",
    )(held)


def solution(mesh):
    return jax.shard_map(
        on_device,
        mesh=mesh,
        in_specs=(
            P(("row", "col"), None, None),
            P(("row", "col"), None),
            P(("row", "col"), None),
            P(),
            P(),
        ),
        out_specs=P("row", None, "col", None),
        check_vma=False,
    )
```

time: 97.6 us -> 37.7 us (0.39)
  local copies, waits for them, and re-layouts: 44 us -> 1.67 us
  Pallas kernels: 0 us -> 34.5 us
  matrix products: 16.4 us -> 0 us
  waiting for transfers between devices: 15.3 us -> 0 us
  other arithmetic: 10.8 us -> 1.34 us
  starting transfers between devices: 8.67 us -> 0 us
  between operations: 1.45 us -> 0.02 us
    pallas_call x0 -> x2, Pallas kernels: none -> 34.5 us  [the longest x1 31 us: on_device(): pl.pallas_call(functools.partial(exchange_kernel, n_row, n_col, group), o...]
    gather x9 -> x0, local copies, waits for them, and re-layouts: 18.5 us -> none  [the longest x8 14.2 us: gather_rows(): return blocks[picks].reshape(-1, blocks.shape[2])]
    dot_general x5 -> x0, matrix products: 16.4 us -> none  [the longest x1 7.27 us: on_device(): jnp.einsum('kab,kbm->kam', stiffness, picked, preferred_element_type=jnp....]
    all_to_all x1 -> x0, waiting for transfers between devices: 12.3 us -> none  [on_device(): lax.all_to_all(pieces, 'col', split_axis=1, concat_axis=1, tiled=True)]
    unnamed x9 -> x2, local copies, waits for them, and re-layouts: 10.7 us -> 0.99 us
    dot_general x1 -> x0, local copies, waits for them, and re-layouts: 8.36 us -> none  [on_device(): jnp.einsum('kab,kbm->kam', stiffness, picked, preferred_element_type=jnp....]
    all_to_all x1 -> x0, starting transfers between devices: 5.93 us -> none  [on_device(): lax.all_to_all(pieces, 'col', split_axis=1, concat_axis=1, tiled=True)]
    scatter-add x1 -> x0, other arithmetic: 5.01 us -> none  [on_device(): return stored.at[local_index, global_index].add(received, mode='drop')]
  transfers between devices with their start and end apart: 3 -> 0, of which waited for: 2 -> 0; matrix products, arithmetic and copies ran while one was open for 17% -> 0% of each run, Pallas kernels for 0% -> 0%
where the time goes in v1:
time: 37.7 us; the launch traced here: 37.5 us
  Pallas kernels  34.5 us (92%)
  local copies, waits for them, and re-layouts  1.67 us (4%)
  other arithmetic  1.34 us (4%)
    pallas_call x1, Pallas kernels, on_device(): pl.pallas_call(functools.partial(exchange_kernel, n_row, n_col, group), o...  31 us
    pallas_call x1, Pallas kernels, on_device(): pl.pallas_call(functools.partial(place_kernel, n_row, n_col), out_shape=j...  3.49 us
    reduce_max x1, other arithmetic, on_device(): table = jnp.max(jnp.where(match, number[None, :] + 1, 0), axis=1)  1.26 us
    unnamed x2, local copies, waits for them, and re-layouts  0.99 us

profile of v1, /device:TPU:0, one launch (start us, length us, event | category | flops | bytes accessed | tf_op | source)
XLA Modules:
  0.0 37.5 jit_solution(17277254412526273179)
XLA Ops:
  0.0 0.7 %slice_bitcast_fusion = s32[28]{0:T(128)S(1)} fusion(s32[28,2]{0,1:T(2,128)} %param.6), kind=kLoop, calls=%fused_computation.5 | loop fusion | bytes 224 | tf_op jit(solution)/shard_map/squeeze | solution.py:209
  0.7 0.1 pad_add_fusion
  0.8 1.3 %select_reduce_fusion.table = s32[44]{0:T(128)} fusion(s32[28]{0:T(128)S(1)} %iota_add_fusion, s32[44]{0:T(128)} %constant.1.clone.1, s32[44]{0:T(128)S(1)} %pad_add_fusion, s32[28]{0:T(128)S(1)} %slice_bitcast_fusion), kind=kLoop, calls=%fused_computation | loop fusion | flops 6116 | bytes 752 | tf_op jit(solution)/shard_map/reduce_max | solution.py:214
  2.0 31.0 %exchange.1.held = bf16[3,8,32,256]{3,2,1,0:T(8,128)(2,1)} custom-call(s32[44]{0:T(128)} %select_reduce_fusion.table, s32[2,28]{1,0:T(2,128)} %bitcast.8, s32[2,32]{1,0:T(2,128)} %bitcast.9, s32[2,4,2,32]{3,2,1,0:T(2,128)} %bitcast.7, bf16[28,256,256]{2,1,0:T(8,128)(2,1)} %stiff_hbm.1, bf16[16,256,256]{2,1,0:T(8,128)(2,1)} %bitcast.6), custom_call_target="tpu_custom_call" | custom-call | tf_op jit(solution)/shard_map/exchange/pallas_call | solution.py:218
  33.0 0.0 copy-start
  33.0 1.0 %copy-done = bf16[3,8,32,256]{3,2,1,0:T(8,128)(2,1)S(1)} copy-done((bf16[3,8,32,256]{3,2,1,0:T(8,128)(2,1)S(1)}, bf16[3,8,32,256]{3,2,1,0:T(8,128)(2,1)}, u32[]{:S(2)}) %copy-start) | copy-done | bytes 393240
  34.0 3.5 %place.1 = bf16[8,32,32,256]{3,2,1,0:T(8,128)(2,1)} custom-call(bf16[3,8,32,256]{3,2,1,0:T(8,128)(2,1)S(1)} %copy-done), custom_call_target="tpu_custom_call" | custom-call | tf_op jit(solution)/shard_map/place/pallas_call | solution.py:253
  (2 shorter events, 0.0 us)
Async XLA Ops:
  33.0 1.0 %copy-start = (bf16[3,8,32,256]{3,2,1,0:T(8,128)(2,1)S(1)}, bf16[3,8,32,256]{3,2,1,0:T(8,128)(2,1)}, u32[]{:S(2)}) copy-start(bf16[3,8,32,256]{3,2,1,0:T(8,128)(2,1)} %exchange.1.held) | copy-start | bytes 1179652

commit v2 on v1

v2 whole, which is shorter than its diff:
```python
import functools

import jax
import jax.numpy as jnp
from jax import lax
from jax.experimental import pallas as pl
from jax.experimental.pallas import tpu as pltpu
from jax.sharding import PartitionSpec as P

MESH = pl.DeviceIdType.MESH
F32 = jnp.float32
BF16 = jnp.bfloat16


def tdot(left, right):
    return lax.dot_general(left, right, (((0,), (0,)), ((), ())), preferred_element_type=F32)


def exchange_kernel(
    n_row, n_col, group,
    index, owner, margin, stiff_hbm, modes_hbm, out,
    stiff, modes, products, sums, applied, far_out, far_in, slots, held, total, before, last,
    stiff_sem, modes_sem, far_send, far_recv, piece_send, piece_recv,
):
    block_total, size, width = stiff.shape
    blocks = modes.shape[0]
    shared = far_out.shape[1]
    my_row = lax.axis_index("row")
    my_col = lax.axis_index("col")
    here = my_row * n_col + my_col
    back = lax.rem(my_row, 2)
    ends = (my_col - 1 + 2 * back, my_row - 1)
    starts = (my_col + 1 - 2 * back, my_row + 1)
    sends = (jnp.logical_and(ends[0] >= 0, ends[0] < n_col), ends[1] >= 0)
    takes = (jnp.logical_and(starts[0] >= 0, starts[0] < n_col), starts[1] < n_row)
    send_first = (here - 1 + back, here - n_col)
    take_first = (here - back, here)
    send_side = (1 - back, 1)
    take_side = (back, 0)
    target = ({"col": jnp.clip(ends[0], 0, n_col - 1)}, {"row": jnp.maximum(ends[1], 0)})
    next_row = {"row": jnp.minimum(starts[1], n_row - 1)}

    modes_copy = pltpu.make_async_copy(modes_hbm, modes, modes_sem)
    modes_copy.start()

    def stiff_copy(c):
        part = pl.ds(c * group, group)
        return pltpu.make_async_copy(stiff_hbm.at[part], stiff.at[part], stiff_sem.at[c])

    def start_stiff(c, carry):
        stiff_copy(c).start()
        return carry

    lax.fori_loop(0, block_total // group, start_stiff, 0)

    barrier = pltpu.get_barrier_semaphore()
    for d in range(1, n_col):
        pl.semaphore_signal(
            barrier, inc=1, device_id={"col": lax.rem(my_col + d, n_col)}, device_id_type=MESH
        )

    @pl.when(sends[1])
    def _():
        pl.semaphore_signal(barrier, inc=1, device_id=target[1], device_id_type=MESH)

    @pl.when(takes[1])
    def _():
        pl.semaphore_signal(barrier, inc=1, device_id=next_row, device_id_type=MESH)

    sums[0] = jnp.zeros((size, width), F32)
    latest = [jnp.int32(0)] * blocks
    for k in range(block_total):
        mine = index[0, k]
        found = jnp.int32(0)
        for a in range(blocks):
            hit = mine == a
            found = jnp.where(hit, latest[a], found)
            latest[a] = jnp.where(hit, k + 1, latest[a])
        before[k] = found
    for a in range(blocks):
        last[a] = latest[a]
    modes_copy.wait()

    def apply_group(c, carry):
        stiff_copy(c).wait()
        for q in range(group):
            k = c * group + q
            products[q] = jnp.dot(stiff[k], modes[index[1, k]], preferred_element_type=F32)
        for q in range(group):
            k = c * group + q
            sums[k + 1] = sums[before[k]] + products[q]
        return carry

    lax.fori_loop(0, block_total // group, apply_group, 0)

    sides = sends[1].astype(jnp.int32) + takes[1].astype(jnp.int32)
    pl.semaphore_wait(barrier, n_col - 1 + sides)

    def far_copy(d, i):
        return pltpu.make_async_remote_copy(
            src_ref=far_out.at[d, i], dst_ref=far_in.at[d, i],
            send_sem=far_send.at[d, i], recv_sem=far_recv.at[d, i],
            device_id=target[d], device_id_type=MESH,
        )

    for d in range(2):
        @pl.when(sends[d])
        def _():
            first = send_first[d]
            flag = owner[d, first]
            for i in range(shared):
                pick = margin[d, i, send_side[d], first]
                far_out[d, i] = jnp.where(
                    flag + send_side[d] == 1, sums[last[pick]].astype(BF16), modes[pick]
                )
                far_copy(d, i).start()

    def piece_copy(slot, d):
        place = my_col - back if slot == 1 else my_col
        peer = lax.rem(my_col + d, n_col)
        return pltpu.make_async_remote_copy(
            src_ref=slots.at[slot, peer], dst_ref=held.at[slot, place],
            send_sem=piece_send.at[slot, d], recv_sem=piece_recv.at[slot, d],
            device_id={"col": peer}, device_id_type=MESH,
        )

    def scatter(slot, value):
        place = my_col - back if slot == 1 else my_col
        slots[slot] = value.astype(BF16).reshape(slots.shape[1:])
        for d in range(1, n_col):
            piece_copy(slot, d).start()
        held[slot, place] = slots[slot, my_col]

    def round_block(a, carry):
        applied[a] = sums[last[a]].astype(BF16)
        return carry

    lax.fori_loop(0, blocks, round_block, 0)
    step = 4 if blocks % 4 == 0 else 1
    total[...] = jnp.zeros_like(total)

    def diagonal_step(c, carry):
        part = pl.ds(c * step, step)
        total[...] += tdot(
            modes[part].reshape(step * size, width), applied[part].reshape(step * size, width)
        )
        return carry

    lax.fori_loop(0, blocks // step, diagonal_step, 0)
    scatter(0, total[...])

    for d in (1, 0):
        @pl.when(takes[d])
        def _():
            first = take_first[d]
            flag = owner[d, first]
            value = None
            for i in range(shared):
                pick = margin[d, i, take_side[d], first]
                near = jnp.where(flag + take_side[d] == 1, applied[pick], modes[pick])
                far_copy(d, i).wait_recv()
                far = far_in[d, i]
                if d == 0:
                    near, far = jnp.where(back == 0, near, far), jnp.where(back == 0, far, near)
                term = tdot(near, far)
                value = term if value is None else value + term
            scatter(d + 1, value)

    @pl.when(jnp.logical_not(takes[1]))
    def _():
        held[2] = jnp.zeros(held.shape[1:], BF16)

    held[1, n_col - 1] = jnp.zeros(held.shape[2:], BF16)

    for d in range(2):
        @pl.when(sends[d])
        def _():
            for i in range(shared):
                far_copy(d, i).wait_send()

    def wait_piece(slot, d):
        source = lax.rem(my_col + n_col - d, n_col)
        place = jnp.clip(source - back, 0, n_col - 1) if slot == 1 else source
        return pltpu.make_async_remote_copy(
            src_ref=slots.at[slot, my_col], dst_ref=held.at[slot, place],
            send_sem=piece_send.at[slot, d], recv_sem=piece_recv.at[slot, d],
            device_id={"col": lax.rem(my_col + d, n_col)}, device_id_type=MESH,
        )

    for d in range(1, n_col):
        wait_piece(0, d).wait_recv()
        piece_copy(0, d).wait_send()

    @pl.when(takes[1])
    def _():
        for d in range(1, n_col):
            wait_piece(2, d).wait_recv()
            piece_copy(2, d).wait_send()

    for d in range(1, n_col):
        origin = lax.rem(my_col + n_col - d, n_col) + 1 - 2 * back

        @pl.when(jnp.logical_and(origin >= 0, origin < n_col))
        def _():
            wait_piece(1, d).wait_recv()

        @pl.when(takes[0])
        def _():
            piece_copy(1, d).wait_send()

    out[...] = held[...]


def place_kernel(n_row, n_col, held_hbm, out, held, zeros, same, after, held_sem, out_sem):
    my_row = lax.axis_index("row")
    fetch = pltpu.make_async_copy(held_hbm, held, held_sem)
    fetch.start()
    zeros[...] = jnp.zeros_like(zeros)

    def write(source, g):
        return pltpu.make_async_copy(source, out.at[:, g], out_sem.at[g])

    for g in range(n_row):
        @pl.when(jnp.logical_and(g != my_row, g != my_row + 1))
        def _():
            write(zeros, g).start()

    same[...] = jnp.zeros_like(same)
    after[...] = jnp.zeros_like(after)
    fetch.wait()
    for i in range(n_col):
        same[i, i] = held[0, i]
        if i < n_col - 1:
            same[i, i + 1] = held[1, i]
    write(same, my_row).start()

    @pl.when(my_row < n_row - 1)
    def _():
        for i in range(n_col):
            after[i, i] = held[2, i]
        write(after, my_row + 1).start()

    for g in range(n_row):
        write(zeros, g).wait()


def on_device(stiffness, stiffness_index, mode_basis, pair_owner, margin):
    n_row = lax.axis_size("row")
    n_col = lax.axis_size("col")
    count, size, _ = stiffness.shape
    width = mode_basis.shape[1]
    blocks = mode_basis.shape[0] // size
    shared = margin.shape[2]
    rows = width // n_col
    group = max(q for q in range(1, 9) if count % q == 0)
    smem = pl.BlockSpec(memory_space=pltpu.SMEM)
    hbm = pl.BlockSpec(memory_space=pl.ANY)
    held = pl.pallas_call(
        functools.partial(exchange_kernel, n_row, n_col, group),
        out_shape=jax.ShapeDtypeStruct((3, n_col, rows, width), BF16),
        in_specs=[smem] * 3 + [hbm] * 2,
        out_specs=pl.BlockSpec(memory_space=pltpu.VMEM),
        scratch_shapes=[
            pltpu.VMEM((count, size, size), BF16),
            pltpu.VMEM((blocks, size, width), BF16),
            pltpu.VMEM((group, size, width), F32),
            pltpu.VMEM((count + 1, size, width), F32),
            pltpu.VMEM((blocks, size, width), BF16),
            pltpu.VMEM((2, shared, size, width), BF16),
            pltpu.VMEM((2, shared, size, width), BF16),
            pltpu.VMEM((3, n_col, rows, width), BF16),
            pltpu.VMEM((3, n_col, rows, width), BF16),
            pltpu.VMEM((width, width), F32),
            pltpu.SMEM((count,), jnp.int32),
            pltpu.SMEM((blocks,), jnp.int32),
            pltpu.SemaphoreType.DMA((count // group,)),
            pltpu.SemaphoreType.DMA,
            pltpu.SemaphoreType.DMA((2, shared)),
            pltpu.SemaphoreType.DMA((2, shared)),
            pltpu.SemaphoreType.DMA((3, n_col)),
            pltpu.SemaphoreType.DMA((3, n_col)),
        ],
        compiler_params=pltpu.CompilerParams(
            collective_id=0, has_side_effects=True, vmem_limit_bytes=56 * 1024 * 1024
        ),
        name="exchange",
    )(
        stiffness_index.T,
        pair_owner.T,
        margin.transpose(1, 2, 3, 0),
        stiffness,
        mode_basis.reshape(blocks, size, width),
    )
    part = (n_col, n_col, rows, width)
    coarse = pl.pallas_call(
        functools.partial(place_kernel, n_row, n_col),
        out_shape=jax.ShapeDtypeStruct((n_col, n_row, n_col, rows, width), BF16),
        in_specs=[hbm],
        out_specs=hbm,
        scratch_shapes=[
            pltpu.VMEM((3, n_col, rows, width), BF16),
            pltpu.VMEM(part, BF16),
            pltpu.VMEM(part, BF16),
            pltpu.VMEM(part, BF16),
            pltpu.SemaphoreType.DMA,
            pltpu.SemaphoreType.DMA((n_row,)),
        ],
        compiler_params=pltpu.CompilerParams(vmem_limit_bytes=56 * 1024 * 1024),
        name="place",
    )(held)
    return coarse.reshape(n_col, n_row * n_col, rows, width)


def solution(mesh):
    return jax.shard_map(
        on_device,
        mesh=mesh,
        in_specs=(
            P(("row", "col"), None, None),
            P(("row", "col"), None),
            P(("row", "col"), None),
            P(),
            P(),
        ),
        out_specs=P("row", None, "col", None),
        check_vma=False,
    )
```

time: 37.7 us -> 32.1 us (0.85)
  Pallas kernels: 34.5 us -> 31.9 us
  local copies, waits for them, and re-layouts: 1.67 us -> 0 us
  other arithmetic: 1.34 us -> 0 us
    pallas_call x1, Pallas kernels: 31 us -> 29.4 us  [on_device(): pl.pallas_call(functools.partial(exchange_kernel, n_row, n_col, group), o...]
    reduce_max x1 -> x0, other arithmetic: 1.26 us -> none  [on_device(): table = jnp.max(jnp.where(match, number[None, :] + 1, 0), axis=1)]
    pallas_call x1, Pallas kernels: 3.49 us -> 2.44 us  [on_device(): pl.pallas_call(functools.partial(place_kernel, n_row, n_col), out_shape=j...]
    unnamed x2 -> x0, local copies, waits for them, and re-layouts: 0.99 us -> none
    squeeze x1 -> x0, local copies, waits for them, and re-layouts: 0.68 us -> none  [on_device(): mine = stiffness_index[:, 0]]
where the time goes in v2:
time: 32.1 us; the launch traced here: 31.9 us
  Pallas kernels  31.9 us (99%)
    pallas_call x1, Pallas kernels, on_device(): pl.pallas_call(functools.partial(exchange_kernel, n_row, n_col, group), o...  29.4 us
    pallas_call x1, Pallas kernels, on_device(): pl.pallas_call(functools.partial(place_kernel, n_row, n_col), out_shape=j...  2.44 us

profile of v2, /device:TPU:0, one launch (start us, length us, event | category | flops | bytes accessed | tf_op | source)
XLA Modules:
  0.0 31.9 jit_solution(12982286694437612061)
XLA Ops:
  0.0 29.4 %exchange.1.held_hbm = bf16[3,8,32,256]{3,2,1,0:T(8,128)(2,1)} custom-call(s32[2,28]{1,0:T(2,128)} %bitcast.7, s32[2,32]{1,0:T(2,128)} %bitcast.8, s32[2,4,2,32]{3,2,1,0:T(2,128)} %bitcast.6, bf16[28,256,256]{2,1,0:T(8,128)(2,1)} %stiff_hbm.1, bf16[16,256,256]{2,1,0:T(8,128)(2,1)} %bitcast.5), custom_call_target="tpu_custom_call" | custom-call | tf_op jit(solution)/shard_map/exchange/pallas_call | solution.py:258
  29.4 2.4 %place.1 = bf16[8,4,8,32,256]{4,3,2,1,0:T(8,128)(2,1)} custom-call(bf16[3,8,32,256]{3,2,1,0:T(8,128)(2,1)} %exchange.1.held_hbm), custom_call_target="tpu_custom_call" | custom-call | tf_op jit(solution)/shard_map/place/pallas_call | solution.py:295

commit v3 on v2

--- a/solution.py
+++ b/solution.py
@@ -17,14 +17,15 @@
 
 
 def exchange_kernel(
-    n_row, n_col, group,
+    n_row, n_col, group, passes,
     index, owner, margin, stiff_hbm, modes_hbm, out,
     stiff, modes, products, sums, applied, far_out, far_in, slots, held, total, before, last,
     stiff_sem, modes_sem, far_send, far_recv, piece_send, piece_recv,
 ):
     block_total, size, width = stiff.shape
     blocks = modes.shape[0]
-    shared = far_out.shape[1]
+    shared = far_out.shape[1] // passes
+    half = size // passes
     my_row = lax.axis_index("row")
     my_col = lax.axis_index("col")
     here = my_row * n_col + my_col
@@ -43,15 +44,15 @@
     modes_copy = pltpu.make_async_copy(modes_hbm, modes, modes_sem)
     modes_copy.start()
 
-    def stiff_copy(c):
-        part = pl.ds(c * group, group)
-        return pltpu.make_async_copy(stiff_hbm.at[part], stiff.at[part], stiff_sem.at[c])
-
-    def start_stiff(c, carry):
-        stiff_copy(c).start()
-        return carry
-
-    lax.fori_loop(0, block_total // group, start_stiff, 0)
+    chunks = block_total // group
+
+    def stiff_copy(h, c):
+        part = (pl.ds(c * group, group), pl.ds(h * half, half))
+        return pltpu.make_async_copy(stiff_hbm.at[part], stiff.at[part], stiff_sem.at[h, c])
+
+    for h in range(passes):
+        for c in range(chunks):
+            stiff_copy(h, c).start()
 
     barrier = pltpu.get_barrier_semaphore()
     for d in range(1, n_col):
@@ -81,39 +82,46 @@
         last[a] = latest[a]
     modes_copy.wait()
 
-    def apply_group(c, carry):
-        stiff_copy(c).wait()
-        for q in range(group):
-            k = c * group + q
-            products[q] = jnp.dot(stiff[k], modes[index[1, k]], preferred_element_type=F32)
-        for q in range(group):
-            k = c * group + q
-            sums[k + 1] = sums[before[k]] + products[q]
-        return carry
-
-    lax.fori_loop(0, block_total // group, apply_group, 0)
+    def far_copy(d, j):
+        return pltpu.make_async_remote_copy(
+            src_ref=far_out.at[d, j], dst_ref=far_in.at[d, j],
+            send_sem=far_send.at[d, j], recv_sem=far_recv.at[d, j],
+            device_id=target[d], device_id_type=MESH,
+        )
 
     sides = sends[1].astype(jnp.int32) + takes[1].astype(jnp.int32)
-    pl.semaphore_wait(barrier, n_col - 1 + sides)
-
-    def far_copy(d, i):
-        return pltpu.make_async_remote_copy(
-            src_ref=far_out.at[d, i], dst_ref=far_in.at[d, i],
-            send_sem=far_send.at[d, i], recv_sem=far_recv.at[d, i],
-            device_id=target[d], device_id_type=MESH,
-        )
-
-    for d in range(2):
-        @pl.when(sends[d])
-        def _():
-            first = send_first[d]
-            flag = owner[d, first]
-            for i in range(shared):
-                pick = margin[d, i, send_side[d], first]
-                far_out[d, i] = jnp.where(
-                    flag + send_side[d] == 1, sums[last[pick]].astype(BF16), modes[pick]
+    for h in range(passes):
+        rows = pl.ds(h * half, half)
+
+        def apply_group(c, carry):
+            stiff_copy(h, c).wait()
+            for q in range(group):
+                k = c * group + q
+                products[q] = jnp.dot(
+                    stiff[k, rows], modes[index[1, k]], preferred_element_type=F32
                 )
-                far_copy(d, i).start()
+            for q in range(group):
+                k = c * group + q
+                sums[k + 1, rows] = sums[before[k], rows] + products[q]
+            return carry
+
+        lax.fori_loop(0, chunks, apply_group, 0)
+        if h == 0:
+            pl.semaphore_wait(barrier, n_col - 1 + sides)
+        for d in range(2):
+            @pl.when(sends[d])
+            def _():
+                first = send_first[d]
+                flag = owner[d, first]
+                for i in range(shared):
+                    pick = margin[d, i, send_side[d], first]
+                    j = h * shared + i
+                    far_out[d, j] = jnp.where(
+                        flag + send_side[d] == 1,
+                        sums[last[pick], rows].astype(BF16),
+                        modes[pick, rows],
+                    )
+                    far_copy(d, j).start()
 
     def piece_copy(slot, d):
         place = my_col - back if slot == 1 else my_col
@@ -155,11 +163,15 @@
             first = take_first[d]
             flag = owner[d, first]
             value = None
-            for i in range(shared):
+            for j in range(passes * shared):
+                h, i = divmod(j, shared)
+                rows = pl.ds(h * half, half)
                 pick = margin[d, i, take_side[d], first]
-                near = jnp.where(flag + take_side[d] == 1, applied[pick], modes[pick])
-                far_copy(d, i).wait_recv()
-                far = far_in[d, i]
+                near = jnp.where(
+                    flag + take_side[d] == 1, applied[pick, rows], modes[pick, rows]
+                )
+                far_copy(d, j).wait_recv()
+                far = far_in[d, j]
                 if d == 0:
                     near, far = jnp.where(back == 0, near, far), jnp.where(back == 0, far, near)
                 term = tdot(near, far)
@@ -175,8 +187,8 @@
     for d in range(2):
         @pl.when(sends[d])
         def _():
-            for i in range(shared):
-                far_copy(d, i).wait_send()
+            for j in range(passes * shared):
+                far_copy(d, j).wait_send()
 
     def wait_piece(slot, d):
         source = lax.rem(my_col + n_col - d, n_col)
@@ -211,10 +223,8 @@
     out[...] = held[...]
 
 
-def place_kernel(n_row, n_col, held_hbm, out, held, zeros, same, after, held_sem, out_sem):
+def place_kernel(n_row, n_col, held, out, zeros, same, after, out_sem):
     my_row = lax.axis_index("row")
-    fetch = pltpu.make_async_copy(held_hbm, held, held_sem)
-    fetch.start()
     zeros[...] = jnp.zeros_like(zeros)
 
     def write(source, g):
@@ -227,7 +237,6 @@
 
     same[...] = jnp.zeros_like(same)
     after[...] = jnp.zeros_like(after)
-    fetch.wait()
     for i in range(n_col):
         same[i, i] = held[0, i]
         if i < n_col - 1:
@@ -254,34 +263,36 @@
     rows = width // n_col
     group = max(q for q in range(1, 9) if count % q == 0)
     smem = pl.BlockSpec(memory_space=pltpu.SMEM)
-    hbm = pl.BlockSpec(memory_space=pl.ANY)
+    hbm = pl.BlockSpec(memory_space=pltpu.HBM)
+    vmem = pl.BlockSpec(memory_space=pltpu.VMEM)
+    passes = 2
     held = pl.pallas_call(
-        functools.partial(exchange_kernel, n_row, n_col, group),
+        functools.partial(exchange_kernel, n_row, n_col, group, passes),
         out_shape=jax.ShapeDtypeStruct((3, n_col, rows, width), BF16),
         in_specs=[smem] * 3 + [hbm] * 2,
         out_specs=pl.BlockSpec(memory_space=pltpu.VMEM),
         scratch_shapes=[
             pltpu.VMEM((count, size, size), BF16),
             pltpu.VMEM((blocks, size, width), BF16),
-            pltpu.VMEM((group, size, width), F32),
+            pltpu.VMEM((group, size // passes, width), F32),
             pltpu.VMEM((count + 1, size, width), F32),
             pltpu.VMEM((blocks, size, width), BF16),
-            pltpu.VMEM((2, shared, size, width), BF16),
-            pltpu.VMEM((2, shared, size, width), BF16),
+            pltpu.VMEM((2, passes * shared, size // passes, width), BF16),
+            pltpu.VMEM((2, passes * shared, size // passes, width), BF16),
             pltpu.VMEM((3, n_col, rows, width), BF16),
             pltpu.VMEM((3, n_col, rows, width), BF16),
             pltpu.VMEM((width, width), F32),
             pltpu.SMEM((count,), jnp.int32),
             pltpu.SMEM((blocks,), jnp.int32),
-            pltpu.SemaphoreType.DMA((count // group,)),
+            pltpu.SemaphoreType.DMA((passes, count // group)),
             pltpu.SemaphoreType.DMA,
-            pltpu.SemaphoreType.DMA((2, shared)),
-            pltpu.SemaphoreType.DMA((2, shared)),
+            pltpu.SemaphoreType.DMA((2, passes * shared)),
+            pltpu.SemaphoreType.DMA((2, passes * shared)),
             pltpu.SemaphoreType.DMA((3, n_col)),
             pltpu.SemaphoreType.DMA((3, n_col)),
         ],
         compiler_params=pltpu.CompilerParams(
-            collective_id=0, has_side_effects=True, vmem_limit_bytes=56 * 1024 * 1024
+            collective_id=0, has_side_effects=True, vmem_limit_bytes=53 * 1024 * 1024
         ),
         name="exchange",
     )(
@@ -295,17 +306,15 @@
     coarse = pl.pallas_call(
         functools.partial(place_kernel, n_row, n_col),
         out_shape=jax.ShapeDtypeStruct((n_col, n_row, n_col, rows, width), BF16),
-        in_specs=[hbm],
+        in_specs=[vmem],
         out_specs=hbm,
         scratch_shapes=[
-            pltpu.VMEM((3, n_col, rows, width), BF16),
             pltpu.VMEM(part, BF16),
             pltpu.VMEM(part, BF16),
             pltpu.VMEM(part, BF16),
-            pltpu.SemaphoreType.DMA,
             pltpu.SemaphoreType.DMA((n_row,)),
         ],
-        compiler_params=pltpu.CompilerParams(vmem_limit_bytes=56 * 1024 * 1024),
+        compiler_params=pltpu.CompilerParams(vmem_limit_bytes=53 * 1024 * 1024),
         name="place",
     )(held)
     return coarse.reshape(n_col, n_row * n_col, rows, width)

time: 32.1 us -> 33.2 us (1.034)
  local copies, waits for them, and re-layouts: 0 us -> 2.05 us
  Pallas kernels: 31.9 us -> 31 us
    unnamed x0 -> x6, local copies, waits for them, and re-layouts: none -> 2.05 us
    pallas_call x1, Pallas kernels: 29.4 us -> 28.8 us  [on_device(): pl.pallas_call(functools.partial(exchange_kernel, n_row, n_col, group, pa...]
where the time goes in v3:
time: 33.2 us; the launch traced here: 33 us
  Pallas kernels  31 us (93%)
  local copies, waits for them, and re-layouts  2.05 us (6%)
    pallas_call x1, Pallas kernels, on_device(): pl.pallas_call(functools.partial(exchange_kernel, n_row, n_col, group, pa...  28.8 us
    pallas_call x1, Pallas kernels, on_device(): pl.pallas_call(functools.partial(place_kernel, n_row, n_col), out_shape=j...  2.11 us
    unnamed x6, local copies, waits for them, and re-layouts  2.05 us

profile of v3, /device:TPU:0, one launch (start us, length us, event | category | flops | bytes accessed | tf_op | source)
XLA Modules:
  0.0 33.0 jit_solution(8809368485217954394)
XLA Ops:
  0.0 0.0 copy-start
  0.0 0.7 %copy-done = s32[32,2,4,2]{0,3,2,1:T(2,128)S(1)} copy-done((s32[32,2,4,2]{0,3,2,1:T(2,128)S(1)}, s32[32,2,4,2]{0,3,2,1:T(2,128)}, u32[]{:S(2)}) %copy-start) | copy-done | bytes 2072
  0.7 0.0 copy-start.1
  0.7 0.7 %copy-done.1 = s32[28,2]{0,1:T(2,128)S(1)} copy-done((s32[28,2]{0,1:T(2,128)S(1)}, s32[28,2]{0,1:T(2,128)}, u32[]{:S(2)}) %copy-start.1) | copy-done | bytes 248
  1.4 0.0 copy-start.2
  1.4 0.7 %copy-done.2 = s32[32,2]{0,1:T(2,128)S(1)} copy-done((s32[32,2]{0,1:T(2,128)S(1)}, s32[32,2]{0,1:T(2,128)}, u32[]{:S(2)}) %copy-start.2) | copy-done | bytes 280
  2.1 28.8 %exchange.1.held = bf16[3,8,32,256]{3,2,1,0:T(8,128)(2,1)S(1)} custom-call(s32[2,28]{1,0:T(2,128)S(1)} %bitcast.6, s32[2,32]{1,0:T(2,128)S(1)} %bitcast.7, s32[2,4,2,32]{3,2,1,0:T(2,128)S(1)} %bitcast.5, bf16[28,256,256]{2,1,0:T(8,128)(2,1)} %stiff_hbm.1, bf16[16,256,256]{2,1,0:T(8,128)(2,1)} %bitcast.8), custom_call_target="tpu_custom_call" | custom-call | tf_op jit(solution)/shard_map/exchange/pallas_call | solution.py:269
  30.9 2.1 %place.1 = bf16[8,4,8,32,256]{4,3,2,1,0:T(8,128)(2,1)} custom-call(bf16[3,8,32,256]{3,2,1,0:T(8,128)(2,1)S(1)} %exchange.1.held), custom_call_target="tpu_custom_call" | custom-call | tf_op jit(solution)/shard_map/place/pallas_call | solution.py:306
Async XLA Ops:
  0.0 0.7 %copy-start = (s32[32,2,4,2]{0,3,2,1:T(2,128)S(1)}, s32[32,2,4,2]{0,3,2,1:T(2,128)}, u32[]{:S(2)}) copy-start(s32[32,2,4,2]{0,3,2,1:T(2,128)} %param.9) | copy-start | bytes 6148
  0.7 0.7 %copy-start.1 = (s32[28,2]{0,1:T(2,128)S(1)}, s32[28,2]{0,1:T(2,128)}, u32[]{:S(2)}) copy-start(s32[28,2]{0,1:T(2,128)} %param.6) | copy-start | bytes 676
  1.4 0.7 %copy-start.2 = (s32[32,2]{0,1:T(2,128)S(1)}, s32[32,2]{0,1:T(2,128)}, u32[]{:S(2)}) copy-start(s32[32,2]{0,1:T(2,128)} %param.8) | copy-start | bytes 772

commit v4 on v3

--- a/solution.py
+++ b/solution.py
@@ -25,7 +25,7 @@
     block_total, size, width = stiff.shape
     blocks = modes.shape[0]
     shared = far_out.shape[1] // passes
-    half = size // passes
+    half = width // passes
     my_row = lax.axis_index("row")
     my_col = lax.axis_index("col")
     here = my_row * n_col + my_col
@@ -46,13 +46,12 @@
 
     chunks = block_total // group
 
-    def stiff_copy(h, c):
-        part = (pl.ds(c * group, group), pl.ds(h * half, half))
-        return pltpu.make_async_copy(stiff_hbm.at[part], stiff.at[part], stiff_sem.at[h, c])
-
-    for h in range(passes):
-        for c in range(chunks):
-            stiff_copy(h, c).start()
+    def stiff_copy(c):
+        part = pl.ds(c * group, group)
+        return pltpu.make_async_copy(stiff_hbm.at[part], stiff.at[part], stiff_sem.at[c])
+
+    for c in range(chunks):
+        stiff_copy(c).start()
 
     barrier = pltpu.get_barrier_semaphore()
     for d in range(1, n_col):
@@ -91,18 +90,19 @@
 
     sides = sends[1].astype(jnp.int32) + takes[1].astype(jnp.int32)
     for h in range(passes):
-        rows = pl.ds(h * half, half)
+        cols = pl.ds(h * half, half)
 
         def apply_group(c, carry):
-            stiff_copy(h, c).wait()
+            if h == 0:
+                stiff_copy(c).wait()
             for q in range(group):
                 k = c * group + q
                 products[q] = jnp.dot(
-                    stiff[k, rows], modes[index[1, k]], preferred_element_type=F32
+                    stiff[k], modes[index[1, k], :, cols], preferred_element_type=F32
                 )
             for q in range(group):
                 k = c * group + q
-                sums[k + 1, rows] = sums[before[k], rows] + products[q]
+                sums[k + 1, :, cols] = sums[before[k], :, cols] + products[q]
             return carry
 
         lax.fori_loop(0, chunks, apply_group, 0)
@@ -118,13 +118,12 @@
                     j = h * shared + i
                     far_out[d, j] = jnp.where(
                         flag + send_side[d] == 1,
-                        sums[last[pick], rows].astype(BF16),
-                        modes[pick, rows],
+                        sums[last[pick], :, cols].astype(BF16),
+                        modes[pick, :, cols],
                     )
                     far_copy(d, j).start()
 
-    def piece_copy(slot, d):
-        place = my_col - back if slot == 1 else my_col
+    def piece_copy(slot, d, place):
         peer = lax.rem(my_col + d, n_col)
         return pltpu.make_async_remote_copy(
             src_ref=slots.at[slot, peer], dst_ref=held.at[slot, place],
@@ -132,12 +131,19 @@
             device_id={"col": peer}, device_id_type=MESH,
         )
 
-    def scatter(slot, value):
-        place = my_col - back if slot == 1 else my_col
-        slots[slot] = value.astype(BF16).reshape(slots.shape[1:])
+    def part_copy(h, d, place):
+        peer = lax.rem(my_col + d, n_col)
+        cols = pl.ds(h * half, half)
+        return pltpu.make_async_remote_copy(
+            src_ref=slots.at[1, peer, :, cols], dst_ref=held.at[1, place, :, cols],
+            send_sem=piece_send.at[1 + 2 * h, d], recv_sem=piece_recv.at[1 + 2 * h, d],
+            device_id={"col": peer}, device_id_type=MESH,
+        )
+
+    def scatter(slot):
         for d in range(1, n_col):
-            piece_copy(slot, d).start()
-        held[slot, place] = slots[slot, my_col]
+            piece_copy(slot, d, my_col).start()
+        held[slot, my_col] = slots[slot, my_col]
 
     def round_block(a, carry):
         applied[a] = sums[last[a]].astype(BF16)
@@ -155,28 +161,59 @@
         return carry
 
     lax.fori_loop(0, blocks // step, diagonal_step, 0)
-    scatter(0, total[...])
-
-    for d in (1, 0):
-        @pl.when(takes[d])
-        def _():
-            first = take_first[d]
-            flag = owner[d, first]
-            value = None
-            for j in range(passes * shared):
-                h, i = divmod(j, shared)
-                rows = pl.ds(h * half, half)
-                pick = margin[d, i, take_side[d], first]
-                near = jnp.where(
-                    flag + take_side[d] == 1, applied[pick, rows], modes[pick, rows]
-                )
-                far_copy(d, j).wait_recv()
-                far = far_in[d, j]
-                if d == 0:
-                    near, far = jnp.where(back == 0, near, far), jnp.where(back == 0, far, near)
-                term = tdot(near, far)
-                value = term if value is None else value + term
-            scatter(d + 1, value)
+    slots[0] = total[...].astype(BF16).reshape(slots.shape[1:])
+    scatter(0)
+
+    def pair_part(d, h, near_left):
+        first = take_first[d]
+        flag = owner[d, first]
+        value = None
+        for i in range(shared):
+            pick = margin[d, i, take_side[d], first]
+            near = jnp.where(flag + take_side[d] == 1, applied[pick], modes[pick])
+            far = far_in[d, h * shared + i]
+            term = tdot(near, far) if near_left else tdot(far, near)
+            value = term if value is None else value + term
+        return value.astype(BF16)
+
+    def wait_far(d, h):
+        for i in range(shared):
+            far_copy(d, h * shared + i).wait_recv()
+
+    @pl.when(takes[1])
+    def _():
+        for h in range(passes):
+            wait_far(1, h)
+            slots[2, :, :, pl.ds(h * half, half)] = pair_part(1, h, True).reshape(
+                n_col, slots.shape[2], half
+            )
+        scatter(2)
+
+    per = n_col // passes
+    for h in range(passes):
+        @pl.when(jnp.logical_and(takes[0], back == 0))
+        def _():
+            wait_far(0, h)
+            cols = pl.ds(h * half, half)
+            slots[1, :, :, cols] = pair_part(0, h, True).reshape(n_col, slots.shape[2], half)
+            for d in range(1, n_col):
+                part_copy(h, d, my_col).start()
+            held[1, my_col, :, cols] = slots[1, my_col, :, cols]
+
+        @pl.when(jnp.logical_and(takes[0], back == 1))
+        def _():
+            wait_far(0, h)
+            slots[1, pl.ds(h * per, per)] = pair_part(0, h, False).reshape(
+                per, slots.shape[2], width
+            )
+            for d in range(1, n_col):
+                @pl.when(lax.rem(my_col + d, n_col) // per == h)
+                def _():
+                    piece_copy(1, d, my_col - 1).start()
+
+            @pl.when(my_col // per == h)
+            def _():
+                held[1, my_col - 1] = slots[1, my_col]
 
     @pl.when(jnp.logical_not(takes[1]))
     def _():
@@ -190,41 +227,46 @@
             for j in range(passes * shared):
                 far_copy(d, j).wait_send()
 
-    def wait_piece(slot, d):
+    for d in range(1, n_col):
         source = lax.rem(my_col + n_col - d, n_col)
-        place = jnp.clip(source - back, 0, n_col - 1) if slot == 1 else source
-        return pltpu.make_async_remote_copy(
-            src_ref=slots.at[slot, my_col], dst_ref=held.at[slot, place],
-            send_sem=piece_send.at[slot, d], recv_sem=piece_recv.at[slot, d],
-            device_id={"col": lax.rem(my_col + d, n_col)}, device_id_type=MESH,
-        )
+        piece_copy(0, d, source).wait_recv()
+        piece_copy(0, d, my_col).wait_send()
+
+    @pl.when(takes[1])
+    def _():
+        for d in range(1, n_col):
+            source = lax.rem(my_col + n_col - d, n_col)
+            piece_copy(2, d, source).wait_recv()
+            piece_copy(2, d, my_col).wait_send()
 
     for d in range(1, n_col):
-        wait_piece(0, d).wait_recv()
-        piece_copy(0, d).wait_send()
-
-    @pl.when(takes[1])
-    def _():
-        for d in range(1, n_col):
-            wait_piece(2, d).wait_recv()
-            piece_copy(2, d).wait_send()
-
-    for d in range(1, n_col):
-        origin = lax.rem(my_col + n_col - d, n_col) + 1 - 2 * back
-
-        @pl.when(jnp.logical_and(origin >= 0, origin < n_col))
-        def _():
-            wait_piece(1, d).wait_recv()
-
-        @pl.when(takes[0])
-        def _():
-            piece_copy(1, d).wait_send()
+        source = lax.rem(my_col + n_col - d, n_col)
+
+        @pl.when(jnp.logical_and(back == 0, source < n_col - 1))
+        def _():
+            for h in range(passes):
+                part_copy(h, d, source).wait_recv()
+
+        @pl.when(jnp.logical_and(back == 1, source > 0))
+        def _():
+            piece_copy(1, d, source - 1).wait_recv()
+
+        @pl.when(jnp.logical_and(takes[0], back == 0))
+        def _():
+            for h in range(passes):
+                part_copy(h, d, my_col).wait_send()
+
+        @pl.when(jnp.logical_and(takes[0], back == 1))
+        def _():
+            piece_copy(1, d, my_col - 1).wait_send()
 
     out[...] = held[...]
 
 
-def place_kernel(n_row, n_col, held, out, zeros, same, after, out_sem):
+def place_kernel(n_row, n_col, held_hbm, out, held, zeros, same, after, held_sem, out_sem):
     my_row = lax.axis_index("row")
+    fetch = pltpu.make_async_copy(held_hbm, held, held_sem)
+    fetch.start()
     zeros[...] = jnp.zeros_like(zeros)
 
     def write(source, g):
@@ -237,6 +279,7 @@
 
     same[...] = jnp.zeros_like(same)
     after[...] = jnp.zeros_like(after)
+    fetch.wait()
     for i in range(n_col):
         same[i, i] = held[0, i]
         if i < n_col - 1:
@@ -263,8 +306,7 @@
     rows = width // n_col
     group = max(q for q in range(1, 9) if count % q == 0)
     smem = pl.BlockSpec(memory_space=pltpu.SMEM)
-    hbm = pl.BlockSpec(memory_space=pltpu.HBM)
-    vmem = pl.BlockSpec(memory_space=pltpu.VMEM)
+    hbm = pl.BlockSpec(memory_space=pl.ANY)
     passes = 2
     held = pl.pallas_call(
         functools.partial(exchange_kernel, n_row, n_col, group, passes),
@@ -274,25 +316,25 @@
         scratch_shapes=[
             pltpu.VMEM((count, size, size), BF16),
             pltpu.VMEM((blocks, size, width), BF16),
-            pltpu.VMEM((group, size // passes, width), F32),
+            pltpu.VMEM((group, size, width // passes), F32),
             pltpu.VMEM((count + 1, size, width), F32),
             pltpu.VMEM((blocks, size, width), BF16),
-            pltpu.VMEM((2, passes * shared, size // passes, width), BF16),
-            pltpu.VMEM((2, passes * shared, size // passes, width), BF16),
+            pltpu.VMEM((2, passes * shared, size, width // passes), BF16),
+            pltpu.VMEM((2, passes * shared, size, width // passes), BF16),
             pltpu.VMEM((3, n_col, rows, width), BF16),
             pltpu.VMEM((3, n_col, rows, width), BF16),
             pltpu.VMEM((width, width), F32),
             pltpu.SMEM((count,), jnp.int32),
             pltpu.SMEM((blocks,), jnp.int32),
-            pltpu.SemaphoreType.DMA((passes, count // group)),
+            pltpu.SemaphoreType.DMA((count // group,)),
             pltpu.SemaphoreType.DMA,
             pltpu.SemaphoreType.DMA((2, passes * shared)),
             pltpu.SemaphoreType.DMA((2, passes * shared)),
-            pltpu.SemaphoreType.DMA((3, n_col)),
-            pltpu.SemaphoreType.DMA((3, n_col)),
+            pltpu.SemaphoreType.DMA((4, n_col)),
+            pltpu.SemaphoreType.DMA((4, n_col)),
         ],
         compiler_params=pltpu.CompilerParams(
-            collective_id=0, has_side_effects=True, vmem_limit_bytes=53 * 1024 * 1024
+            collective_id=0, has_side_effects=True, vmem_limit_bytes=56 * 1024 * 1024
         ),
         name="exchange",
     )(
@@ -306,15 +348,17 @@
     coarse = pl.pallas_call(
         functools.partial(place_kernel, n_row, n_col),
         out_shape=jax.ShapeDtypeStruct((n_col, n_row, n_col, rows, width), BF16),
-        in_specs=[vmem],
+        in_specs=[hbm],
         out_specs=hbm,
         scratch_shapes=[
+            pltpu.VMEM((3, n_col, rows, width), BF16),
             pltpu.VMEM(part, BF16),
             pltpu.VMEM(part, BF16),
             pltpu.VMEM(part, BF16),
+            pltpu.SemaphoreType.DMA,
             pltpu.SemaphoreType.DMA((n_row,)),
         ],
-        compiler_params=pltpu.CompilerParams(vmem_limit_bytes=53 * 1024 * 1024),
+        compiler_params=pltpu.CompilerParams(vmem_limit_bytes=56 * 1024 * 1024),
         name="place",
     )(held)
     return coarse.reshape(n_col, n_row * n_col, rows, width)

time: 33.2 us -> 32.8 us (0.988)
  local copies, waits for them, and re-layouts: 2.05 us -> 0 us
  Pallas kernels: 31 us -> 32.6 us
    unnamed x6 -> x0, local copies, waits for them, and re-layouts: 2.05 us -> none
    pallas_call x1, Pallas kernels: 28.8 us -> 30.2 us  [on_device(): pl.pallas_call(functools.partial(exchange_kernel, n_row, n_col, group, pa...]
where the time goes in v4:
time: 32.8 us; the launch traced here: 32.6 us
  Pallas kernels  32.6 us (99%)
    pallas_call x1, Pallas kernels, on_device(): pl.pallas_call(functools.partial(exchange_kernel, n_row, n_col, group, pa...  30.2 us
    pallas_call x1, Pallas kernels, on_device(): pl.pallas_call(functools.partial(place_kernel, n_row, n_col), out_shape=j...  2.44 us

profile of v4, /device:TPU:0, one launch (start us, length us, event | category | flops | bytes accessed | tf_op | source)
XLA Modules:
  0.0 32.6 jit_solution(12149086585864528456)
XLA Ops:
  0.0 30.2 %exchange.1.held_hbm = bf16[3,8,32,256]{3,2,1,0:T(8,128)(2,1)} custom-call(s32[2,28]{1,0:T(2,128)} %bitcast.7, s32[2,32]{1,0:T(2,128)} %bitcast.8, s32[2,4,2,32]{3,2,1,0:T(2,128)} %bitcast.6, bf16[28,256,256]{2,1,0:T(8,128)(2,1)} %stiff_hbm.1, bf16[16,256,256]{2,1,0:T(8,128)(2,1)} %bitcast.5), custom_call_target="tpu_custom_call" | custom-call | tf_op jit(solution)/shard_map/exchange/pallas_call | solution.py:311
  30.2 2.4 %place.1 = bf16[8,4,8,32,256]{4,3,2,1,0:T(8,128)(2,1)} custom-call(bf16[3,8,32,256]{3,2,1,0:T(8,128)(2,1)} %exchange.1.held_hbm), custom_call_target="tpu_custom_call" | custom-call | tf_op jit(solution)/shard_map/place/pallas_call | solution.py:348

commit v5 on v2

--- a/solution.py
+++ b/solution.py
@@ -81,17 +81,20 @@
         last[a] = latest[a]
     modes_copy.wait()
 
-    def apply_group(c, carry):
-        stiff_copy(c).wait()
-        for q in range(group):
-            k = c * group + q
-            products[q] = jnp.dot(stiff[k], modes[index[1, k]], preferred_element_type=F32)
-        for q in range(group):
-            k = c * group + q
-            sums[k + 1] = sums[before[k]] + products[q]
-        return carry
-
-    lax.fori_loop(0, block_total // group, apply_group, 0)
+    slot_count = products.shape[0]
+
+    def add_product(k):
+        sums[k + 1] = sums[before[k]] + products[k % slot_count]
+
+    for k in range(block_total):
+        if k % group == 0:
+            stiff_copy(k // group).wait()
+        products[k % slot_count] = jnp.dot(
+            stiff[k], modes[index[1, k]], preferred_element_type=F32
+        )
+        if k > 0:
+            add_product(k - 1)
+    add_product(block_total - 1)
 
     sides = sends[1].astype(jnp.int32) + takes[1].astype(jnp.int32)
     pl.semaphore_wait(barrier, n_col - 1 + sides)
@@ -263,7 +266,7 @@
         scratch_shapes=[
             pltpu.VMEM((count, size, size), BF16),
             pltpu.VMEM((blocks, size, width), BF16),
-            pltpu.VMEM((group, size, width), F32),
+            pltpu.VMEM((4, size, width), F32),
             pltpu.VMEM((count + 1, size, width), F32),
             pltpu.VMEM((blocks, size, width), BF16),
             pltpu.VMEM((2, shared, size, width), BF16),

time: 32.1 us -> 32.3 us (level)
  no operation moved by 1% of the time
where the time goes in v5:
time: 32.3 us; the launch traced here: 32.1 us
  Pallas kernels  32.1 us (99%)
    pallas_call x1, Pallas kernels, on_device(): pl.pallas_call(functools.partial(exchange_kernel, n_row, n_col, group), o...  29.6 us
    pallas_call x1, Pallas kernels, on_device(): pl.pallas_call(functools.partial(place_kernel, n_row, n_col), out_shape=j...  2.44 us

profile of v5, /device:TPU:0, one launch (start us, length us, event | category | flops | bytes accessed | tf_op | source)
XLA Modules:
  0.0 32.1 jit_solution(3692592660222003156)
XLA Ops:
  0.0 29.6 %exchange.1.held_hbm = bf16[3,8,32,256]{3,2,1,0:T(8,128)(2,1)} custom-call(s32[2,28]{1,0:T(2,128)} %bitcast.7, s32[2,32]{1,0:T(2,128)} %bitcast.8, s32[2,4,2,32]{3,2,1,0:T(2,128)} %bitcast.6, bf16[28,256,256]{2,1,0:T(8,128)(2,1)} %stiff_hbm.1, bf16[16,256,256]{2,1,0:T(8,128)(2,1)} %bitcast.5), custom_call_target="tpu_custom_call" | custom-call | tf_op jit(solution)/shard_map/exchange/pallas_call | solution.py:261
  29.6 2.4 %place.1 = bf16[8,4,8,32,256]{4,3,2,1,0:T(8,128)(2,1)} custom-call(bf16[3,8,32,256]{3,2,1,0:T(8,128)(2,1)} %exchange.1.held_hbm), custom_call_target="tpu_custom_call" | custom-call | tf_op jit(solution)/shard_map/place/pallas_call | solution.py:298

commit v6 on v3

--- a/solution.py
+++ b/solution.py
@@ -223,8 +223,10 @@
     out[...] = held[...]
 
 
-def place_kernel(n_row, n_col, held, out, zeros, same, after, out_sem):
+def place_kernel(n_row, n_col, held_hbm, out, held, zeros, same, after, held_sem, out_sem):
     my_row = lax.axis_index("row")
+    fetch = pltpu.make_async_copy(held_hbm, held, held_sem)
+    fetch.start()
     zeros[...] = jnp.zeros_like(zeros)
 
     def write(source, g):
@@ -237,6 +239,7 @@
 
     same[...] = jnp.zeros_like(same)
     after[...] = jnp.zeros_like(after)
+    fetch.wait()
     for i in range(n_col):
         same[i, i] = held[0, i]
         if i < n_col - 1:
@@ -263,8 +266,7 @@
     rows = width // n_col
     group = max(q for q in range(1, 9) if count % q == 0)
     smem = pl.BlockSpec(memory_space=pltpu.SMEM)
-    hbm = pl.BlockSpec(memory_space=pltpu.HBM)
-    vmem = pl.BlockSpec(memory_space=pltpu.VMEM)
+    hbm = pl.BlockSpec(memory_space=pl.ANY)
     passes = 2
     held = pl.pallas_call(
         functools.partial(exchange_kernel, n_row, n_col, group, passes),
@@ -292,7 +294,7 @@
             pltpu.SemaphoreType.DMA((3, n_col)),
         ],
         compiler_params=pltpu.CompilerParams(
-            collective_id=0, has_side_effects=True, vmem_limit_bytes=53 * 1024 * 1024
+            collective_id=0, has_side_effects=True, vmem_limit_bytes=56 * 1024 * 1024
         ),
         name="exchange",
     )(
@@ -306,15 +308,17 @@
     coarse = pl.pallas_call(
         functools.partial(place_kernel, n_row, n_col),
         out_shape=jax.ShapeDtypeStruct((n_col, n_row, n_col, rows, width), BF16),
-        in_specs=[vmem],
+        in_specs=[hbm],
         out_specs=hbm,
         scratch_shapes=[
+            pltpu.VMEM((3, n_col, rows, width), BF16),
             pltpu.VMEM(part, BF16),
             pltpu.VMEM(part, BF16),
             pltpu.VMEM(part, BF16),
+            pltpu.SemaphoreType.DMA,
             pltpu.SemaphoreType.DMA((n_row,)),
         ],
-        compiler_params=pltpu.CompilerParams(vmem_limit_bytes=53 * 1024 * 1024),
+        compiler_params=pltpu.CompilerParams(vmem_limit_bytes=56 * 1024 * 1024),
         name="place",
     )(held)
     return coarse.reshape(n_col, n_row * n_col, rows, width)

time: 33.2 us -> 32.4 us (0.976)
  local copies, waits for them, and re-layouts: 2.05 us -> 0 us
  Pallas kernels: 31 us -> 32.1 us
    unnamed x6 -> x0, local copies, waits for them, and re-layouts: 2.05 us -> none
    pallas_call x1, Pallas kernels: 28.8 us -> 29.7 us  [on_device(): pl.pallas_call(functools.partial(exchange_kernel, n_row, n_col, group, pa...]
where the time goes in v6:
time: 32.4 us; the launch traced here: 32.2 us
  Pallas kernels  32.1 us (99%)
    pallas_call x1, Pallas kernels, on_device(): pl.pallas_call(functools.partial(exchange_kernel, n_row, n_col, group, pa...  29.7 us
    pallas_call x1, Pallas kernels, on_device(): pl.pallas_call(functools.partial(place_kernel, n_row, n_col), out_shape=j...  2.44 us

profile of v6, /device:TPU:0, one launch (start us, length us, event | category | flops | bytes accessed | tf_op | source)
XLA Modules:
  0.0 32.2 jit_solution(2994335390881253938)
XLA Ops:
  0.0 29.7 %exchange.1.held_hbm = bf16[3,8,32,256]{3,2,1,0:T(8,128)(2,1)} custom-call(s32[2,28]{1,0:T(2,128)} %bitcast.7, s32[2,32]{1,0:T(2,128)} %bitcast.8, s32[2,4,2,32]{3,2,1,0:T(2,128)} %bitcast.6, bf16[28,256,256]{2,1,0:T(8,128)(2,1)} %stiff_hbm.1, bf16[16,256,256]{2,1,0:T(8,128)(2,1)} %bitcast.5), custom_call_target="tpu_custom_call" | custom-call | tf_op jit(solution)/shard_map/exchange/pallas_call | solution.py:271
  29.7 2.4 %place.1 = bf16[8,4,8,32,256]{4,3,2,1,0:T(8,128)(2,1)} custom-call(bf16[3,8,32,256]{3,2,1,0:T(8,128)(2,1)} %exchange.1.held_hbm), custom_call_target="tpu_custom_call" | custom-call | tf_op jit(solution)/shard_map/place/pallas_call | solution.py:308
